TPU v7x, 512 devices: a whole 4x4x16 slice. The times are simulated.
512 devices in a mesh: group: 8 (over y, core), member: 64 (over x, z).
Axes of the slice: x: 4, y: 4, z: 16, core: 2. Of those that a mesh axis runs over, the one named last changes fastest.
Arguments:
- state: float32 [8192, 64, 128], P(('group', 'member')), may hold values from -2.5 to 2.5
- blocks: bfloat16 [8192, 6, 128, 128], P(('group', 'member')), may hold values from -1 to 1
- rate: float32 [8192, 128], P(('group', 'member')), may hold values from 0.1 to 1
- own_col: int32 [8192], P(('group', 'member')), may hold values from 0 to 15
- member_col: int32 [8192, 4], P(('group', 'member')), may hold values from 0 to 63, as said below
- group_col: int32 [8192, 1], P(('group', 'member')), may hold values from 0 to 15, as said below
- member_send: int32 [512, 64], P(('group', 'member')), may hold values from 0 to 15
- group_send: int32 [512, 16], P(('group', 'member')), may hold values from 0 to 15
Outputs:
- new_state: float32 [8192, 64, 128], P(('group', 'member'))
Inputs may be any that keep to these rules, and one draw needn't show every extreme that they name: `member_col`: on each device the 64 entries of its rows name every member index equally often. `group_col`: on each device the 16 entries of its rows name every slot equally often.
All inputs are finite; a program needn't handle non-finite values.
Results may differ from a plain program's by a relative error of at most 0.00092.
Values may be sent and summed in bfloat16 or wider, within the bound.
A program may use at most 64 MiB of HBM per device.

v0:
```python
import jax
import jax.numpy as jnp
from jax import lax
from jax.sharding import PartitionSpec as P

STEPS = 2


step_size = 0.1


def per_device(state, blocks, rate, own_col, member_col, group_col, member_send, group_send):
    members = member_col.shape[1]

    def derivative(field):
        rounded = field.astype(jnp.bfloat16)
        member_out = rounded[member_send[0]]
        group_out = rounded[group_send[0]]
        far_blocks = lax.all_to_all(group_out, "group", split_axis=0, concat_axis=0, tiled=True)
        own_rows = rounded[own_col]
        far_rows = far_blocks[group_col]
        own_term = jnp.einsum(
            "itc,icd->itd", own_rows, blocks[:, 0], preferred_element_type=jnp.float32
        )
        far_term = jnp.einsum(
            "iktc,ikcd->itd", far_rows, blocks[:, 1 + members :], preferred_element_type=jnp.float32
        )
        taken = lax.all_to_all(member_out, "member", split_axis=0, concat_axis=0, tiled=True)[
            member_col
        ]
        near_term = jnp.einsum(
            "iktc,ikcd->itd", taken, blocks[:, 1 : 1 + members], preferred_element_type=jnp.float32
        )
        product = own_term + far_term + near_term
        return -product + rate[:, None, :] * (field - field * field * field)

    current = state
    for step in range(STEPS):
        first = derivative(current)
        second = derivative(current + 0.5 * step_size * first)
        third = derivative(current + 0.5 * step_size * second)
        fourth = derivative(current + step_size * third)
        current = current + step_size / 6.0 * (first + 2.0 * second + 2.0 * third + fourth)
    return current


def solution(mesh):
    return jax.shard_map(
        per_device,
        mesh=mesh,
        in_specs=(
            P(("group", "member"), None, None),
            P(("group", "member"), None, None, None),
            P(("group", "member"), None),
            P(("group", "member")),
            P(("group", "member"), None),
            P(("group", "member"), None),
            P(("group", "member"), None),
            P(("group", "member"), None),
        ),
        out_specs=P(("group", "member"), None, None),
        check_vma=False,
    )
```

profile of v0, /device:TPU:6, one launch (start us, length us, event | category | flops | bytes accessed | tf_op | source)
XLA Modules:
  0.0 648.0 jit_solution(11670045136619148299)
XLA Ops:
  10.0 5.3 all-to-all-done
  15.3 19.0 %all-to-all-start.1 = ((bf16[64,64,128]{2,1,0:T(8,128)(2,1)}), bf16[64,64,128]{2,1,0:T(8,128)(2,1)}, u32[]{:S(2)}, u32[]{:S(2)}) async-start(bf16[64,64,128]{2,1,0:T(8,128)(2,1)} %gather_fusion.3), calls=%async_computation.1 | async-start | bytes 2097152 | tf_op jit(solution)/shard_map/all_to_all | solution.py:28
  41.6 46.0 %all-to-all-done.1 = bf16[64,64,128]{2,1,0:T(8,128)(2,1)} async-done(((bf16[64,64,128]{2,1,0:T(8,128)(2,1)}), bf16[64,64,128]{2,1,0:T(8,128)(2,1)}, u32[]{:S(2)}, u32[]{:S(2)}) %all-to-all-start.1) | async-done | bytes 1048608 | tf_op jit(solution)/shard_map/all_to_all | solution.py:28
  100.4 5.9 all-to-all-done.2
  106.2 7.1 %all-to-all-start.3 = ((bf16[64,64,128]{2,1,0:T(8,128)(2,1)}), bf16[64,64,128]{2,1,0:T(8,128)(2,1)}, u32[]{:S(2)}, u32[]{:S(2)}) async-start(bf16[64,64,128]{2,1,0:T(8,128)(2,1)} %gather_fusion.8), calls=%async_computation.3 | async-start | bytes 2097152 | tf_op jit(solution)/shard_map/all_to_all | solution.py:28
  120.3 46.3 %all-to-all-done.3 = bf16[64,64,128]{2,1,0:T(8,128)(2,1)} async-done(((bf16[64,64,128]{2,1,0:T(8,128)(2,1)}), bf16[64,64,128]{2,1,0:T(8,128)(2,1)}, u32[]{:S(2)}, u32[]{:S(2)}) %all-to-all-start.3) | async-done | bytes 1048608 | tf_op jit(solution)/shard_map/all_to_all | solution.py:28
  179.5 5.9 all-to-all-done.4
  185.4 7.1 %all-to-all-start.5 = ((bf16[64,64,128]{2,1,0:T(8,128)(2,1)}), bf16[64,64,128]{2,1,0:T(8,128)(2,1)}, u32[]{:S(2)}, u32[]{:S(2)}) async-start(bf16[64,64,128]{2,1,0:T(8,128)(2,1)} %gather_fusion.13), calls=%async_computation.5 | async-start | bytes 2097152 | tf_op jit(solution)/shard_map/all_to_all | solution.py:28
  199.5 46.3 %all-to-all-done.5 = bf16[64,64,128]{2,1,0:T(8,128)(2,1)} async-done(((bf16[64,64,128]{2,1,0:T(8,128)(2,1)}), bf16[64,64,128]{2,1,0:T(8,128)(2,1)}, u32[]{:S(2)}, u32[]{:S(2)}) %all-to-all-start.5) | async-done | bytes 1048608 | tf_op jit(solution)/shard_map/all_to_all | solution.py:28
  258.7 5.9 all-to-all-done.6
  264.6 7.1 %all-to-all-start.7 = ((bf16[64,64,128]{2,1,0:T(8,128)(2,1)}), bf16[64,64,128]{2,1,0:T(8,128)(2,1)}, u32[]{:S(2)}, u32[]{:S(2)}) async-start(bf16[64,64,128]{2,1,0:T(8,128)(2,1)} %gather_fusion.18), calls=%async_computation.7 | async-start | bytes 2097152 | tf_op jit(solution)/shard_map/all_to_all | solution.py:28
  278.6 46.3 %all-to-all-done.7 = bf16[64,64,128]{2,1,0:T(8,128)(2,1)} async-done(((bf16[64,64,128]{2,1,0:T(8,128)(2,1)}), bf16[64,64,128]{2,1,0:T(8,128)(2,1)}, u32[]{:S(2)}, u32[]{:S(2)}) %all-to-all-start.7) | async-done | bytes 1048608 | tf_op jit(solution)/shard_map/all_to_all | solution.py:28
  338.2 5.9 all-to-all-done.8
  344.1 7.1 %all-to-all-start.9 = ((bf16[64,64,128]{2,1,0:T(8,128)(2,1)}), bf16[64,64,128]{2,1,0:T(8,128)(2,1)}, u32[]{:S(2)}, u32[]{:S(2)}) async-start(bf16[64,64,128]{2,1,0:T(8,128)(2,1)} %gather_fusion.23), calls=%async_computation.9 | async-start | bytes 2097152 | tf_op jit(solution)/shard_map/all_to_all | solution.py:28
  358.2 46.3 %all-to-all-done.9 = bf16[64,64,128]{2,1,0:T(8,128)(2,1)} async-done(((bf16[64,64,128]{2,1,0:T(8,128)(2,1)}), bf16[64,64,128]{2,1,0:T(8,128)(2,1)}, u32[]{:S(2)}, u32[]{:S(2)}) %all-to-all-start.9) | async-done | bytes 1048608 | tf_op jit(solution)/shard_map/all_to_all | solution.py:28
  417.2 5.9 all-to-all-done.10
  423.1 7.1 %all-to-all-start.11 = ((bf16[64,64,128]{2,1,0:T(8,128)(2,1)}), bf16[64,64,128]{2,1,0:T(8,128)(2,1)}, u32[]{:S(2)}, u32[]{:S(2)}) async-start(bf16[64,64,128]{2,1,0:T(8,128)(2,1)} %gather_fusion.28), calls=%async_computation.11 | async-start | bytes 2097152 | tf_op jit(solution)/shard_map/all_to_all | solution.py:28
  437.2 46.3 %all-to-all-done.11 = bf16[64,64,128]{2,1,0:T(8,128)(2,1)} async-done(((bf16[64,64,128]{2,1,0:T(8,128)(2,1)}), bf16[64,64,128]{2,1,0:T(8,128)(2,1)}, u32[]{:S(2)}, u32[]{:S(2)}) %all-to-all-start.11) | async-done | bytes 1048608 | tf_op jit(solution)/shard_map/all_to_all | solution.py:28
  496.4 5.9 all-to-all-done.12
  502.2 7.1 %all-to-all-start.13 = ((bf16[64,64,128]{2,1,0:T(8,128)(2,1)}), bf16[64,64,128]{2,1,0:T(8,128)(2,1)}, u32[]{:S(2)}, u32[]{:S(2)}) async-start(bf16[64,64,128]{2,1,0:T(8,128)(2,1)} %gather_fusion.33), calls=%async_computation.13 | async-start | bytes 2097152 | tf_op jit(solution)/shard_map/all_to_all | solution.py:28
  516.3 46.3 %all-to-all-done.13 = bf16[64,64,128]{2,1,0:T(8,128)(2,1)} async-done(((bf16[64,64,128]{2,1,0:T(8,128)(2,1)}), bf16[64,64,128]{2,1,0:T(8,128)(2,1)}, u32[]{:S(2)}, u32[]{:S(2)}) %all-to-all-start.13) | async-done | bytes 1048608 | tf_op jit(solution)/shard_map/all_to_all | solution.py:28
  575.5 5.9 all-to-all-done.14
  581.4 7.1 %all-to-all-start.15 = ((bf16[64,64,128]{2,1,0:T(8,128)(2,1)}), bf16[64,64,128]{2,1,0:T(8,128)(2,1)}, u32[]{:S(2)}, u32[]{:S(2)}) async-start(bf16[64,64,128]{2,1,0:T(8,128)(2,1)} %gather_fusion.38), calls=%async_computation.15 | async-start | bytes 2097152 | tf_op jit(solution)/shard_map/all_to_all | solution.py:28
  595.4 46.3 %all-to-all-done.15 = bf16[64,64,128]{2,1,0:T(8,128)(2,1)} async-done(((bf16[64,64,128]{2,1,0:T(8,128)(2,1)}), bf16[64,64,128]{2,1,0:T(8,128)(2,1)}, u32[]{:S(2)}, u32[]{:S(2)}) %all-to-all-start.15) | async-done | bytes 1048608 | tf_op jit(solution)/shard_map/all_to_all | solution.py:28
  (95 shorter events, 162.5 us)
Async XLA Ops:
  0.0 34.3 %copy-start.3 = (s32[16]{0:T(128)S(1)}, s32[16]{0:T(128)}, u32[]{:S(2)}) copy-start(s32[16]{0:T(128)} %param.11) | copy-start | bytes 196
  0.7 35.0 %copy-start.2 = (s32[16,4]{0,1:T(4,128)S(1)}, s32[16,4]{0,1:T(4,128)}, u32[]{:S(2)}) copy-start(s32[16,4]{0,1:T(4,128)} %param.12) | copy-start | bytes 772
  0.7 35.2 %copy-start.4 = (s32[16,1]{0,1:T(1,128)S(1)}, s32[16,1]{0,1:T(1,128)}, u32[]{:S(2)}) copy-start(s32[16,1]{0,1:T(1,128)} %param.13) | copy-start | bytes 196
  0.7 35.2 %copy-start = (bf16[16,6,128,128]{3,2,1,0:T(8,128)(2,1)S(1)}, bf16[16,6,128,128]{3,2,1,0:T(8,128)(2,1)}, u32[]{:S(2)}) copy-start(bf16[16,6,128,128]{3,2,1,0:T(8,128)(2,1)} %param.9) | copy-start | bytes 9437188
  3.2 12.1 %all-to-all-start = ((bf16[16,64,128]{2,1,0:T(8,128)(2,1)}), bf16[16,64,128]{2,1,0:T(8,128)(2,1)}, u32[]{:S(2)}, u32[]{:S(2)}) async-start(bf16[16,64,128]{2,1,0:T(8,128)(2,1)} %gather_fusion.1), calls=%async_computation | async-start | bytes 524288 | tf_op jit(solution)/shard_map/all_to_all | solution.py:19
  15.3 72.3 %all-to-all-start.1 = ((bf16[64,64,128]{2,1,0:T(8,128)(2,1)}), bf16[64,64,128]{2,1,0:T(8,128)(2,1)}, u32[]{:S(2)}, u32[]{:S(2)}) async-start(bf16[64,64,128]{2,1,0:T(8,128)(2,1)} %gather_fusion.3), calls=%async_computation.1 | async-start | bytes 2097152 | tf_op jit(solution)/shard_map/all_to_all | solution.py:28
  34.4 56.1 %copy-start.1 = (f32[16,128]{1,0:T(8,128)S(1)}, f32[16,128]{1,0:T(8,128)}, u32[]{:S(2)}) copy-start(f32[16,128]{1,0:T(8,128)} %param.10) | copy-start | bytes 24580
  94.7 11.6 %all-to-all-start.2 = ((bf16[16,64,128]{2,1,0:T(8,128)(2,1)}), bf16[16,64,128]{2,1,0:T(8,128)(2,1)}, u32[]{:S(2)}, u32[]{:S(2)}) async-start(bf16[16,64,128]{2,1,0:T(8,128)(2,1)} %gather_fusion.6), calls=%async_computation.2 | async-start | bytes 524288 | tf_op jit(solution)/shard_map/all_to_all | solution.py:19
  106.2 60.4 %all-to-all-start.3 = ((bf16[64,64,128]{2,1,0:T(8,128)(2,1)}), bf16[64,64,128]{2,1,0:T(8,128)(2,1)}, u32[]{:S(2)}, u32[]{:S(2)}) async-start(bf16[64,64,128]{2,1,0:T(8,128)(2,1)} %gather_fusion.8), calls=%async_computation.3 | async-start | bytes 2097152 | tf_op jit(solution)/shard_map/all_to_all | solution.py:28
  173.8 11.6 %all-to-all-start.4 = ((bf16[16,64,128]{2,1,0:T(8,128)(2,1)}), bf16[16,64,128]{2,1,0:T(8,128)(2,1)}, u32[]{:S(2)}, u32[]{:S(2)}) async-start(bf16[16,64,128]{2,1,0:T(8,128)(2,1)} %gather_fusion.11), calls=%async_computation.4 | async-start | bytes 524288 | tf_op jit(solution)/shard_map/all_to_all | solution.py:19
  185.4 60.4 %all-to-all-start.5 = ((bf16[64,64,128]{2,1,0:T(8,128)(2,1)}), bf16[64,64,128]{2,1,0:T(8,128)(2,1)}, u32[]{:S(2)}, u32[]{:S(2)}) async-start(bf16[64,64,128]{2,1,0:T(8,128)(2,1)} %gather_fusion.13), calls=%async_computation.5 | async-start | bytes 2097152 | tf_op jit(solution)/shard_map/all_to_all | solution.py:28
  253.0 11.6 %all-to-all-start.6 = ((bf16[16,64,128]{2,1,0:T(8,128)(2,1)}), bf16[16,64,128]{2,1,0:T(8,128)(2,1)}, u32[]{:S(2)}, u32[]{:S(2)}) async-start(bf16[16,64,128]{2,1,0:T(8,128)(2,1)} %gather_fusion.16), calls=%async_computation.6 | async-start | bytes 524288 | tf_op jit(solution)/shard_map/all_to_all | solution.py:19
  264.6 60.4 %all-to-all-start.7 = ((bf16[64,64,128]{2,1,0:T(8,128)(2,1)}), bf16[64,64,128]{2,1,0:T(8,128)(2,1)}, u32[]{:S(2)}, u32[]{:S(2)}) async-start(bf16[64,64,128]{2,1,0:T(8,128)(2,1)} %gather_fusion.18), calls=%async_computation.7 | async-start | bytes 2097152 | tf_op jit(solution)/shard_map/all_to_all | solution.py:28
  332.5 11.6 %all-to-all-start.8 = ((bf16[16,64,128]{2,1,0:T(8,128)(2,1)}), bf16[16,64,128]{2,1,0:T(8,128)(2,1)}, u32[]{:S(2)}, u32[]{:S(2)}) async-start(bf16[16,64,128]{2,1,0:T(8,128)(2,1)} %gather_fusion.21), calls=%async_computation.8 | async-start | bytes 524288 | tf_op jit(solution)/shard_map/all_to_all | solution.py:19
  344.1 60.4 %all-to-all-start.9 = ((bf16[64,64,128]{2,1,0:T(8,128)(2,1)}), bf16[64,64,128]{2,1,0:T(8,128)(2,1)}, u32[]{:S(2)}, u32[]{:S(2)}) async-start(bf16[64,64,128]{2,1,0:T(8,128)(2,1)} %gather_fusion.23), calls=%async_computation.9 | async-start | bytes 2097152 | tf_op jit(solution)/shard_map/all_to_all | solution.py:28
  411.5 11.6 %all-to-all-start.10 = ((bf16[16,64,128]{2,1,0:T(8,128)(2,1)}), bf16[16,64,128]{2,1,0:T(8,128)(2,1)}, u32[]{:S(2)}, u32[]{:S(2)}) async-start(bf16[16,64,128]{2,1,0:T(8,128)(2,1)} %gather_fusion.26), calls=%async_computation.10 | async-start | bytes 524288 | tf_op jit(solution)/shard_map/all_to_all | solution.py:19
  423.1 60.4 %all-to-all-start.11 = ((bf16[64,64,128]{2,1,0:T(8,128)(2,1)}), bf16[64,64,128]{2,1,0:T(8,128)(2,1)}, u32[]{:S(2)}, u32[]{:S(2)}) async-start(bf16[64,64,128]{2,1,0:T(8,128)(2,1)} %gather_fusion.28), calls=%async_computation.11 | async-start | bytes 2097152 | tf_op jit(solution)/shard_map/all_to_all | solution.py:28
  490.7 11.6 %all-to-all-start.12 = ((bf16[16,64,128]{2,1,0:T(8,128)(2,1)}), bf16[16,64,128]{2,1,0:T(8,128)(2,1)}, u32[]{:S(2)}, u32[]{:S(2)}) async-start(bf16[16,64,128]{2,1,0:T(8,128)(2,1)} %gather_fusion.31), calls=%async_computation.12 | async-start | bytes 524288 | tf_op jit(solution)/shard_map/all_to_all | solution.py:19
  502.2 60.4 %all-to-all-start.13 = ((bf16[64,64,128]{2,1,0:T(8,128)(2,1)}), bf16[64,64,128]{2,1,0:T(8,128)(2,1)}, u32[]{:S(2)}, u32[]{:S(2)}) async-start(bf16[64,64,128]{2,1,0:T(8,128)(2,1)} %gather_fusion.33), calls=%async_computation.13 | async-start | bytes 2097152 | tf_op jit(solution)/shard_map/all_to_all | solution.py:28
  569.8 11.6 %all-to-all-start.14 = ((bf16[16,64,128]{2,1,0:T(8,128)(2,1)}), bf16[16,64,128]{2,1,0:T(8,128)(2,1)}, u32[]{:S(2)}, u32[]{:S(2)}) async-start(bf16[16,64,128]{2,1,0:T(8,128)(2,1)} %gather_fusion.36), calls=%async_computation.14 | async-start | bytes 524288 | tf_op jit(solution)/shard_map/all_to_all | solution.py:19
  581.4 60.4 %all-to-all-start.15 = ((bf16[64,64,128]{2,1,0:T(8,128)(2,1)}), bf16[64,64,128]{2,1,0:T(8,128)(2,1)}, u32[]{:S(2)}, u32[]{:S(2)}) async-start(bf16[64,64,128]{2,1,0:T(8,128)(2,1)} %gather_fusion.38), calls=%async_computation.15 | async-start | bytes 2097152 | tf_op jit(solution)/shard_map/all_to_all | solution.py:28
where the time goes:
time: 651 us; the launch traced here: 648 us
  waiting for transfers between devices  417 us (64%)
  starting transfers between devices  101 us (16%)
  local copies, waits for them, and re-layouts  69.4 us (11%)
  matrix products  57.7 us (9%)
    all_to_all x8, waiting for transfers between devices, derivative(): lax.all_to_all(member_out, 'member', split_axis=0, concat_axis=0, tiled=T...  370 us
    all_to_all x8, starting transfers between devices, derivative(): lax.all_to_all(member_out, 'member', split_axis=0, concat_axis=0, tiled=T...  68.6 us
    all_to_all x8, waiting for transfers between devices, derivative(): lax.all_to_all(group_out, 'group', split_axis=0, concat_axis=0, tiled=True)  46.5 us
    all_to_all x8, starting transfers between devices, derivative(): lax.all_to_all(group_out, 'group', split_axis=0, concat_axis=0, tiled=True)  32.8 us
    dot_general x8, matrix products, derivative(): jnp.einsum('iktc,ikcd->itd', taken, blocks[:, 1:1 + members], preferred_e...  24.6 us
    gather x8, local copies, waits for them, and re-layouts, derivative(): lax.all_to_all(member_out, 'member', split_axis=0, concat_axis=0, tiled=T...  23 us
    dot_general x8, matrix products, derivative(): jnp.einsum('iktc,ikcd->itd', far_rows, blocks[:, 1 + members:], preferred...  17 us
    dot_general x8, matrix products, derivative(): jnp.einsum('itc,icd->itd', own_rows, blocks[:, 0], preferred_element_type...  16.2 us
  transfers between devices with their start and end apart: 16, of which 16 were waited for; matrix products, arithmetic and copies ran while one was open for 11% of the time, Pallas kernels for 0%

commit v1 on v0

v1 whole, which is shorter than its diff:
```python
import functools

import jax
import jax.numpy as jnp
from jax import lax
from jax.experimental import pallas as pl
from jax.experimental.pallas import tpu as pltpu
from jax.sharding import PartitionSpec as P

MESH = pl.DeviceIdType.MESH
STEPS = 2
STEP_SIZE = 0.1
EVALS = 4 * STEPS

X = 4
Z = 16
DEPTH = 4
HALVES = 2


def slot_of(back):
    half, base = Z // 2, 2 * DEPTH + 1
    side = half - DEPTH - 1
    up = Z - back
    low = jnp.where(back <= DEPTH, back, base + back - DEPTH - 1)
    high = jnp.where(up <= DEPTH, DEPTH + up, base + side + up - DEPTH - 1)
    return jnp.where(back == half, Z - 1, jnp.where(back < half, low, high))


def kernel(
    groups, rows, per_group,
    table, own_col, group_send, zblk, zsum, gblk, gsum,
    state, blocks, rate,
    out,
    own, field, total, lands, local0, local1, near, far, xin, fpack, gpack, gin,
    zprod, gprod, oprod,
    z_send, z_recv, f_send, f_recv, xn_send, xn_recv, xf_send, xf_recv, g_send, g_recv,
):
    half = Z // 2
    nears = 2 * DEPTH + 1
    side = half - DEPTH - 1
    traj = own.shape[2]
    local = (local0, local1)
    g = lax.axis_index("group")
    m = lax.axis_index("member")
    x, z = m // Z, m % Z

    def at_z(step):
        return (z + step + Z) % Z

    def member(xx, zz):
        return xx * Z + zz

    def along_z(step):
        return (g, member(x, at_z(step)))

    def along_x(step):
        return (g, member((x + step) % X, z))

    partners = [along_z(s * d) for d in range(1, max(1, half - DEPTH) + 1) for s in (1, -1)]
    partners += [along_x(j) for j in range(1, X)]
    partners += [((g + o) % groups, m) for o in range(1, groups)]
    barrier = pltpu.get_barrier_semaphore()
    for partner in partners:
        pl.semaphore_signal(barrier, inc=1, device_id=partner, device_id_type=MESH)
    pl.semaphore_wait(barrier, len(partners))

    def remote(src, dst, send, recv, device):
        return pltpu.make_async_remote_copy(
            src_ref=src, dst_ref=dst, send_sem=send, recv_sem=recv,
            device_id=device, device_id_type=MESH,
        )

    def z_copy(p, h, side_, t):
        src = own.at[h] if t == 0 else lands.at[p, h, side_, t - 1]
        return remote(
            src, lands.at[p, h, side_, t], z_send.at[h, side_, t], z_recv.at[p, h, side_, t],
            along_z(1 if side_ == 0 else -1),
        )

    def f_copy(p, h, side_, d):
        if d == half - DEPTH:
            js = pl.ds(0, X // 2) if side_ == 0 else pl.ds(X // 2, X // 2)
            slot = side * 2
        else:
            js = pl.ds(0, X)
            slot = side_ * side + d - 1
        return remote(
            fpack.at[h, side_, d - 1, js], far.at[p, h, js, slot],
            f_send.at[h, side_, d - 1], f_recv.at[p, h, side_, d - 1],
            along_z(d if side_ == 0 else -d),
        )

    def xn_copy(p, h, j):
        return remote(
            near.at[h, j], xin.at[p, h, j - 1, pl.ds(0, nears)],
            xn_send.at[h, j - 1], xn_recv.at[p, h, j - 1], along_x(j),
        )

    def xf_copy(p, h, j):
        return remote(
            far.at[p, h, j], xin.at[p, h, j - 1, pl.ds(nears, Z - nears)],
            xf_send.at[h, j - 1], xf_recv.at[p, h, j - 1], along_x(j),
        )

    def g_copy(p, h, o):
        return remote(
            gpack.at[h, pl.ds(o * per_group, per_group)],
            gin.at[p, h, pl.ds((o - 1) * per_group, per_group)],
            g_send.at[h, o - 1], g_recv.at[p, h, o - 1], ((g + o) % groups, m),
        )

    def product(left, block):
        return jnp.dot(left, blocks[block], preferred_element_type=jnp.float32)

    def first(h):
        part = slice(h * traj, (h + 1) * traj)

        def row(i, _):
            value = state[i, part, :]
            out[i, part, :] = value
            field[h, i] = value
            own[h, i] = value.astype(jnp.bfloat16)
            return 0

        lax.fori_loop(0, rows, row, 0)

    def begin(e, h):
        p = e % 2
        for side_ in (0, 1):
            z_copy(p, h, side_, 0).start()
        for o in range(groups):
            target = (g + o) % groups
            for s in range(per_group):
                gpack[h, o * per_group + s] = own[h, group_send[target * per_group + s]]
        for o in range(1, groups):
            g_copy(p, h, o).start()
        for j in range(X):
            near[h, j, 0] = own[h, table[m, member((x + j) % X, z)]]

        def products(n, _):
            for i in range(8):
                i = n * 8 + i
                oprod[h, i] = product(own[h, own_col[i]], i * K_ALL)
            return 0

        lax.fori_loop(0, rows // 8, products, 0)

    def step(e, h, t):
        p = e % 2
        for side_ in (0, 1):
            z_copy(p, h, side_, t - 1).wait_recv()
            if t < DEPTH:
                z_copy(p, h, side_, t).start()
            local[side_][...] = lands[p, h, side_, t - 1]
        for side_ in (0, 1):
            back = t if side_ == 0 else -t
            source = member(x, at_z(-back))
            if t == DEPTH:
                for d in range(1, half - DEPTH + 1):
                    js = range(X)
                    if d == half - DEPTH:
                        js = js[: X // 2] if side_ == 0 else js[X // 2 :]
                    there = at_z(d if side_ == 0 else -d)
                    for j in js:
                        fpack[h, side_, d - 1, j] = local[side_][table[source, member((x + j) % X, there)]]
                    f_copy(p, h, side_, d).start()
        for side_ in (0, 1):
            back = t if side_ == 0 else -t
            source = member(x, at_z(-back))
            for j in range(X):
                near[h, j, side_ * DEPTH + t] = local[side_][table[source, member((x + j) % X, z)]]
        if t == DEPTH:
            for j in range(1, X):
                xn_copy(p, h, j).start()

    def group_products(e, h):
        p = e % 2
        for o in range(1, groups):
            g_copy(p, h, o).wait_recv()
        for s in range(per_group):
            gprod[h, s] = product(gpack[h, s], gblk[s])

        def products(n, _):
            for s in range(per_group):
                k = n * per_group + s
                gprod[h, k + per_group] = product(gin[p, h, k], gblk[k + per_group])
            return 0

        lax.fori_loop(0, groups - 1, products, 0)

    def across(e, h):
        p = e % 2
        for side_ in (0, 1):
            for d in range(1, half - DEPTH + 1):
                f_copy(p, h, side_, d).wait_recv()
        for j in range(1, X):
            xf_copy(p, h, j).start()
        for s in range(nears):
            zprod[h, s] = product(near[h, 0, s], zblk[s])
        for s in range(nears, Z):
            zprod[h, s] = product(far[p, h, 0, s - nears], zblk[s])
        for j in range(1, X):
            xn_copy(p, h, j).wait_recv()

        def products(j, _):
            for s in range(nears):
                zprod[h, (j + 1) * Z + s] = product(xin[p, h, j, s], zblk[(j + 1) * Z + s])
            return 0

        lax.fori_loop(0, X - 1, products, 0)

    def finish(e, h):
        p = e % 2
        for j in range(1, X):
            xf_copy(p, h, j).wait_recv()

        def products(j, _):
            for s in range(nears, Z):
                zprod[h, (j + 1) * Z + s] = product(xin[p, h, j, s], zblk[(j + 1) * Z + s])
            return 0

        lax.fori_loop(0, X - 1, products, 0)
        for side_ in (0, 1):
            for t in range(DEPTH):
                z_copy(p, h, side_, t).wait_send()
            for d in range(1, half - DEPTH + 1):
                f_copy(p, h, side_, d).wait_send()
        for j in range(1, X):
            xn_copy(p, h, j).wait_send()
            xf_copy(p, h, j).wait_send()
        for o in range(1, groups):
            g_copy(p, h, o).wait_send()

        part = slice(h * traj, (h + 1) * traj)
        stage = e % 4
        is_first, is_last = stage == 0, stage == 3
        weight = jnp.where(is_first | is_last, 1.0, 2.0).astype(jnp.float32)
        ahead = jnp.where(stage == 2, STEP_SIZE, 0.5 * STEP_SIZE).astype(jnp.float32)
        members = zsum.shape[0] // rows

        def update(i):
            y = oprod[h, i] + gprod[h, gsum[i]]
            for k in range(members):
                y = y + zprod[h, zsum[i * members + k]]
            v = field[h, i]
            u = out[i, part, :]
            slope = rate[pl.ds(i, 1), :] * (v - v * v * v) - y
            before = jnp.where(is_first, 0.0, total[h, i])
            summed = before + weight * slope
            total[h, i] = summed
            value = u + jnp.where(is_last, (STEP_SIZE / 6.0) * summed, ahead * slope)
            out[i, part, :] = jnp.where(is_last, value, u)
            field[h, i] = value
            own[h, i] = value.astype(jnp.bfloat16)

        def four(n, _):
            for i in range(4):
                update(n * 4 + i)
            return 0

        lax.fori_loop(0, rows // 4, four, 0)

    K_ALL = blocks.shape[0] // rows

    first(0)
    first(1)

    def stages(h):
        parts = [lambda e: begin(e, h)]
        for t in range(1, DEPTH + 1):
            parts.append(lambda e, t=t: step(e, h, t))
        parts.append(lambda e: across(e, h))
        return parts

    a, b = stages(0), stages(1)
    cut = (len(a) + 1) // 2

    def evaluation(i, _):
        after = i >= 1
        ahead = i < EVALS

        def late(fn):
            pl.when(after)(lambda: fn(i - 1))

        def now(fn):
            pl.when(ahead)(lambda: fn(i))

        late(lambda e: finish(e, 0))
        for n in range(cut):
            now(a[n])
            if n == 1:
                now(lambda e: group_products(e, 0))
            if cut + n < len(b):
                late(b[cut + n])
        late(lambda e: finish(e, 1))
        for n in range(cut):
            now(b[n])
            if n == 1:
                now(lambda e: group_products(e, 1))
            if cut + n < len(a):
                now(a[cut + n])
        return 0

    lax.fori_loop(0, EVALS + 1, evaluation, 0)


def per_device(groups, state, blocks, rate, own_col, member_col, group_col, member_send, group_send):
    rows, traj, cells = state.shape
    members = member_col.shape[1]
    count = blocks.shape[1]
    per_group = group_send.shape[1] // groups
    part = traj // HALVES
    half, nears = Z // 2, 2 * DEPTH + 1
    g = lax.axis_index("group")
    m = lax.axis_index("member")
    x, z = m // Z, m % Z

    table = lax.all_gather(member_send[0], "member", axis=0)
    col = member_col.reshape(-1)
    zsum = ((x - col // Z + X) % X) * Z + slot_of((z - col % Z + Z) % Z)
    ids = jnp.arange(rows * members, dtype=jnp.int32)
    block_of = (ids // members) * count + 1 + ids % members
    zblk = jnp.sum(jnp.where(zsum[None, :] == ids[:, None], block_of[None, :], 0), axis=1)
    gcol = group_col.reshape(-1)
    gsum = ((g - gcol // per_group + groups) % groups) * per_group + gcol % per_group
    gids = jnp.arange(gcol.shape[0], dtype=jnp.int32)
    gblock = gids * count + count - 1
    gblk = jnp.sum(jnp.where(gsum[None, :] == gids[:, None], gblock[None, :], 0), axis=1)

    smem = pl.BlockSpec(memory_space=pltpu.SMEM)
    vmem = pl.BlockSpec(memory_space=pltpu.VMEM)
    bf, f32 = jnp.bfloat16, jnp.float32
    tile = (part, cells)
    dma = pltpu.SemaphoreType.DMA
    return pl.pallas_call(
        functools.partial(kernel, groups, rows, per_group),
        out_shape=jax.ShapeDtypeStruct(state.shape, f32),
        in_specs=[smem] * 7 + [vmem] * 3,
        out_specs=vmem,
        scratch_shapes=[
            pltpu.VMEM((HALVES, rows) + tile, bf),
            pltpu.VMEM((HALVES, rows) + tile, f32),
            pltpu.VMEM((HALVES, rows) + tile, f32),
            pltpu.VMEM((2, HALVES, 2, DEPTH, rows) + tile, bf),
            pltpu.VMEM((rows,) + tile, bf),
            pltpu.VMEM((rows,) + tile, bf),
            pltpu.VMEM((HALVES, X, nears) + tile, bf),
            pltpu.VMEM((2, HALVES, X, Z - nears) + tile, bf),
            pltpu.VMEM((2, HALVES, X - 1, Z) + tile, bf),
            pltpu.VMEM((HALVES, 2, half - DEPTH, X) + tile, bf),
            pltpu.VMEM((HALVES, groups * per_group) + tile, bf),
            pltpu.VMEM((2, HALVES, (groups - 1) * per_group) + tile, bf),
            pltpu.VMEM((HALVES, X * Z) + tile, f32),
            pltpu.VMEM((HALVES, groups * per_group) + tile, f32),
            pltpu.VMEM((HALVES, rows) + tile, f32),
            dma((HALVES, 2, DEPTH)),
            dma((2, HALVES, 2, DEPTH)),
            dma((HALVES, 2, half - DEPTH)),
            dma((2, HALVES, 2, half - DEPTH)),
            dma((HALVES, X - 1)),
            dma((2, HALVES, X - 1)),
            dma((HALVES, X - 1)),
            dma((2, HALVES, X - 1)),
            dma((HALVES, groups - 1)),
            dma((2, HALVES, groups - 1)),
        ],
        compiler_params=pltpu.CompilerParams(
            collective_id=0, has_side_effects=True, vmem_limit_bytes=48 * 2**20
        ),
        cost_estimate=pl.CostEstimate(
            flops=EVALS * 2 * rows * count * traj * cells * cells,
            bytes_accessed=4 * 2**20, transcendentals=0,
        ),
    )(
        table, own_col, group_send[0], zblk.astype(jnp.int32), zsum.astype(jnp.int32),
        gblk.astype(jnp.int32), gsum.astype(jnp.int32),
        state, blocks.reshape(rows * count, cells, cells), rate,
    )


def solution(mesh):
    return jax.shard_map(
        functools.partial(per_device, mesh.shape["group"]),
        mesh=mesh,
        in_specs=(
            P(("group", "member"), None, None),
            P(("group", "member"), None, None, None),
            P(("group", "member"), None),
            P(("group", "member")),
            P(("group", "member"), None),
            P(("group", "member"), None),
            P(("group", "member"), None),
            P(("group", "member"), None),
        ),
        out_specs=P(("group", "member"), None, None),
        check_vma=False,
    )
```

time: 651 us -> 463 us (0.71)
  waiting for transfers between devices: 417 us -> 0 us
  Pallas kernels: 0 us -> 376 us
  starting transfers between devices: 101 us -> 0 us
  blocking collectives: 0 us -> 78.7 us
  local copies, waits for them, and re-layouts: 69.4 us -> 6.58 us
  matrix products: 57.7 us -> 0 us
    all_to_all x16 -> x0, waiting for transfers between devices: 417 us -> none  [the longest x8 370 us: derivative(): lax.all_to_all(member_out, 'member', split_axis=0, concat_axis=0, tiled=T...]
    pallas_call x0 -> x1, Pallas kernels: none -> 376 us  [per_device(): pl.pallas_call(functools.partial(kernel, groups, rows, per_group), out_sh...]
    all_to_all x16 -> x0, starting transfers between devices: 101 us -> none  [the longest x8 68.6 us: derivative(): lax.all_to_all(member_out, 'member', split_axis=0, concat_axis=0, tiled=T...]
    all_gather x0 -> x1, blocking collectives: none -> 78.7 us  [per_device(): table = lax.all_gather(member_send[0], 'member', axis=0)]
    gather x40 -> x0, local copies, waits for them, and re-layouts: 69.2 us -> none  [the longest x8 23 us: derivative(): lax.all_to_all(member_out, 'member', split_axis=0, concat_axis=0, tiled=T...]
    dot_general x24 -> x0, matrix products: 57.7 us -> none  [the longest x8 24.6 us: derivative(): jnp.einsum('iktc,ikcd->itd', taken, blocks[:, 1:1 + members], preferred_e...]
  transfers between devices with their start and end apart: 16 -> 0, of which waited for: 16 -> 0; matrix products, arithmetic and copies ran while one was open for 11% -> 0% of each run, Pallas kernels for 0% -> 0%
where the time goes in v1:
time: 463 us; the launch traced here: 462 us
  Pallas kernels  376 us (81%)
  blocking collectives  78.7 us (17%)
  local copies, waits for them, and re-layouts  6.58 us (1%)
    pallas_call x1, Pallas kernels, per_device(): pl.pallas_call(functools.partial(kernel, groups, rows, per_group), out_sh...  376 us
    all_gather x1, blocking collectives, per_device(): table = lax.all_gather(member_send[0], 'member', axis=0)  78.7 us

profile of v1, /device:TPU:6, one launch (start us, length us, event | category | flops | bytes accessed | tf_op | source)
XLA Modules:
  0.0 461.8 jit_solution(10802656569485770514)
XLA Ops:
  0.0 0.7 fusion.1
  0.7 0.1 select_reduce_fusion.1.gblk
  0.8 0.8 copy.14
  1.6 0.1 reshape.190
  1.7 0.1 select_reduce_fusion.zblk
  1.8 78.7 %all-gather = s32[64,1,64]{2,1,0:T(1,128)S(1)} all-gather(s32[1,1,64]{2,1,0:T(1,128)} %bitcast.20), channel_id=1, replica_groups=mesh['group'=8,'member'=64] {'member'}, dimensions={0}, use_global_device_ids=true | all-gather | bytes 16640 | tf_op jit(solution)/shard_map/all_gather | solution.py:319
  80.5 0.0 copy-start
  80.5 1.9 copy-done
  82.4 0.0 copy-start.1
  82.4 1.0 copy-done.1
  83.4 0.0 copy-start.2
  83.4 0.7 copy-done.2
  84.1 0.0 copy-start.3
  84.1 0.7 copy-done.3
  84.8 0.0 copy-start.4
  84.8 0.7 copy-done.4
  85.4 375.6 %shard_map.82 = f32[16,64,128]{2,1,0:T(8,128)S(1)} custom-call(s32[64,64]{1,0:T(8,128)S(1)} %bitcast.17, s32[16]{0:T(128)S(1)} %copy-done.3, s32[16]{0:T(128)S(1)} %bitcast.19, s32[64]{0:T(128)S(1)} %select_reduce_fusion.zblk, s32[64]{0:T(128)S(1)} %get-tuple-element.6.zsum, s32[16]{0:T(128)S(1)} %select_reduce_fusion.1.gblk, s32[16]{0:T(128)S(1)} %get-tuple-element.7.gsum, ...), custom_call_target="tpu_custom_call" | custom-call | flops 1610612736 | bytes 4194304 | tf_op jit(solution)/shard_map/pallas_call | solution.py:336
  461.0 0.8 copy.16
  (1 shorter events, 0.0 us)
Async XLA Ops:
  80.5 1.9 copy-start
  82.4 1.0 copy-start.1
  83.4 0.7 copy-start.2
  84.1 0.7 copy-start.3
  84.8 0.7 copy-start.4

commit v2 on v1

v2 whole, which is shorter than its diff:
```python
import functools

import jax
import jax.numpy as jnp
from jax import lax
from jax.experimental import pallas as pl
from jax.experimental.pallas import tpu as pltpu
from jax.sharding import PartitionSpec as P

MESH = pl.DeviceIdType.MESH
STEPS = 2
STEP_SIZE = 0.1
EVALS = 4 * STEPS

X = 4
Z = 16
DEPTH = 3
PARTS = 4
ORDER = (("turn", 0), ("3", 2), ("across", 3), ("2", 1), ("1", 0), ("group", 0))


def slot_of(back):
    half, base = Z // 2, 2 * DEPTH + 1
    side = half - DEPTH - 1
    up = Z - back
    low = jnp.where(back <= DEPTH, back, base + back - DEPTH - 1)
    high = jnp.where(up <= DEPTH, DEPTH + up, base + side + up - DEPTH - 1)
    return jnp.where(back == half, Z - 1, jnp.where(back < half, low, high))


def kernel(
    groups, rows, per_group,
    numbers, own_table, state, blocks_in, rate,
    out,
    blocks, table_in, table, table_send, table_recv, load_sem,
    own, field, total, lands, local0, local1, near, far, xin, fpack, gpack, gin,
    zprod, gprod, oprod,
    z_send, z_recv, f_send, f_recv, xn_send, xn_recv, xf_send, xf_recv, g_send, g_recv,
):
    half = Z // 2
    nears = 2 * DEPTH + 1
    count = blocks.shape[0] // rows
    side = half - DEPTH - 1
    traj = own.shape[2]
    local = (local0, local1)
    g = lax.axis_index("group")
    m = lax.axis_index("member")
    x, z = m // Z, m % Z

    def at_z(step):
        return (z + step + Z) % Z

    def member(xx, zz):
        return xx * Z + zz

    def along_z(step):
        return (g, member(x, at_z(step)))

    def along_x(step):
        return (g, member((x + step) % X, z))

    reach = max(DEPTH, half - DEPTH)
    partners = [along_z(s * d) for d in range(1, reach + 1) for s in (1, -1)]
    partners += [along_x(j) for j in range(1, X)]
    partners += [((g + o) % groups, m) for o in range(1, groups)]
    load = pltpu.make_async_copy(blocks_in, blocks, load_sem.at[0])
    load.start()
    barrier = pltpu.get_barrier_semaphore()
    for partner in partners:
        pl.semaphore_signal(barrier, inc=1, device_id=partner, device_id_type=MESH)
    pl.semaphore_wait(barrier, len(partners))

    def remote(src, dst, send, recv, device):
        return pltpu.make_async_remote_copy(
            src_ref=src, dst_ref=dst, send_sem=send, recv_sem=recv,
            device_id=device, device_id_type=MESH,
        )

    def table_copy(side_, t):
        slot = side_ * DEPTH + t - 1
        return remote(
            own_table, table_in.at[slot], table_send.at[slot], table_recv.at[slot],
            along_z(t if side_ == 0 else -t),
        )

    members = X * Z // rows
    zblk_at = 0
    zsum_at = zblk_at + X * Z
    gblk_at = zsum_at + X * Z
    gsum_at = gblk_at + groups * per_group
    own_at = gsum_at + rows
    gsend_at = own_at + rows
    send_at = gsend_at + groups * per_group

    def picked(side_, t, to):
        return table[side_ * DEPTH + t - 1, 0, to]

    def z_copy(p, h, side_, t):
        src = own.at[h] if t == 0 else lands.at[p, h, side_, t - 1]
        return remote(
            src, lands.at[p, h, side_, t], z_send.at[h, side_, t], z_recv.at[p, h, side_, t],
            along_z(1 if side_ == 0 else -1),
        )

    def f_copy(p, h, side_, d):
        if d == half - DEPTH:
            js = pl.ds(0, X // 2) if side_ == 0 else pl.ds(X // 2, X // 2)
            slot = side * 2
        else:
            js = pl.ds(0, X)
            slot = side_ * side + d - 1
        return remote(
            fpack.at[h, side_, d - 1, js], far.at[p, h, js, slot],
            f_send.at[h, side_, d - 1], f_recv.at[p, h, side_, d - 1],
            along_z(d if side_ == 0 else -d),
        )

    def xn_copy(p, h, j):
        return remote(
            near.at[h, j], xin.at[p, h, j - 1, pl.ds(0, nears)],
            xn_send.at[h, j - 1], xn_recv.at[p, h, j - 1], along_x(j),
        )

    def xf_copy(p, h, j):
        return remote(
            far.at[p, h, j], xin.at[p, h, j - 1, pl.ds(nears, Z - nears)],
            xf_send.at[h, j - 1], xf_recv.at[p, h, j - 1], along_x(j),
        )

    def g_copy(p, h, o):
        return remote(
            gpack.at[h, pl.ds(o * per_group, per_group)],
            gin.at[p, h, pl.ds((o - 1) * per_group, per_group)],
            g_send.at[h, o - 1], g_recv.at[p, h, o - 1], ((g + o) % groups, m),
        )

    def product(left, block):
        return jnp.dot(left, blocks[block], preferred_element_type=jnp.float32)

    def part_of(h):
        return pl.ds(pl.multiple_of(h * traj, traj), traj)

    def first(h):
        part = part_of(h)

        def row(i, _):
            value = state[i, part, :]
            out[i, part, :] = value
            field[h, i] = value
            own[h, i] = value.astype(jnp.bfloat16)
            return 0

        lax.fori_loop(0, rows, row, 0)

    def launch(e, h):
        for side_ in (0, 1):
            z_copy(e % 2, h, side_, 0).start()

    def begin(e, h):
        p = e % 2
        for o in range(groups):
            target = (g + o) % groups
            for s in range(per_group):
                gpack[h, o * per_group + s] = own[h, numbers[gsend_at + target * per_group + s]]
        for o in range(1, groups):
            g_copy(p, h, o).start()
        for j in range(X):
            near[h, j, 0] = own[h, numbers[send_at + member((x + j) % X, z)]]

        def products(n, _):
            for i in range(8):
                i = n * 8 + i
                oprod[h, i] = product(own[h, numbers[own_at + i]], i * count)
            return 0

        lax.fori_loop(0, rows // 8, products, 0)

    def step(e, h, t):
        p = e % 2
        for side_ in (0, 1):
            z_copy(p, h, side_, t - 1).wait_recv()
            if t < DEPTH:
                z_copy(p, h, side_, t).start()
            local[side_][...] = lands[p, h, side_, t - 1]
        for side_ in (0, 1):
            if t == DEPTH:
                for d in range(1, half - DEPTH + 1):
                    js = range(X)
                    if d == half - DEPTH:
                        js = js[: X // 2] if side_ == 0 else js[X // 2 :]
                    there = at_z(d if side_ == 0 else -d)
                    for j in js:
                        fpack[h, side_, d - 1, j] = local[side_][picked(side_, t, member((x + j) % X, there))]
                    f_copy(p, h, side_, d).start()
        for side_ in (0, 1):
            for j in range(X):
                near[h, j, side_ * DEPTH + t] = local[side_][picked(side_, t, member((x + j) % X, z))]
        if t == DEPTH:
            for j in range(1, X):
                xn_copy(p, h, j).start()

    def group_products(e, h):
        p = e % 2
        for o in range(1, groups):
            g_copy(p, h, o).wait_recv()
        for s in range(per_group):
            gprod[h, s] = product(gpack[h, s], numbers[gblk_at + s])

        def products(n, _):
            for s in range(per_group):
                k = n * per_group + s
                gprod[h, k + per_group] = product(gin[p, h, k], numbers[gblk_at + k + per_group])
            return 0

        lax.fori_loop(0, groups - 1, products, 0)

    def across(e, h):
        p = e % 2
        for side_ in (0, 1):
            for d in range(1, half - DEPTH + 1):
                f_copy(p, h, side_, d).wait_recv()
        for j in range(1, X):
            xf_copy(p, h, j).start()
        for s in range(nears):
            zprod[h, s] = product(near[h, 0, s], numbers[zblk_at + s])
        for s in range(nears, Z):
            zprod[h, s] = product(far[p, h, 0, s - nears], numbers[zblk_at + s])
        for j in range(1, X):
            xn_copy(p, h, j).wait_recv()

        def products(j, _):
            for s in range(nears):
                zprod[h, (j + 1) * Z + s] = product(xin[p, h, j, s], numbers[zblk_at + (j + 1) * Z + s])
            return 0

        lax.fori_loop(0, X - 1, products, 0)

    def finish(e, h):
        p = e % 2
        for j in range(1, X):
            xf_copy(p, h, j).wait_recv()

        def products(j, _):
            for s in range(nears, Z):
                zprod[h, (j + 1) * Z + s] = product(xin[p, h, j, s], numbers[zblk_at + (j + 1) * Z + s])
            return 0

        lax.fori_loop(0, X - 1, products, 0)
        for side_ in (0, 1):
            for t in range(DEPTH):
                z_copy(p, h, side_, t).wait_send()
            for d in range(1, half - DEPTH + 1):
                f_copy(p, h, side_, d).wait_send()
        for j in range(1, X):
            xn_copy(p, h, j).wait_send()
            xf_copy(p, h, j).wait_send()
        for o in range(1, groups):
            g_copy(p, h, o).wait_send()

        part = part_of(h)
        stage = e % 4
        is_first, is_last = stage == 0, stage == 3
        weight = jnp.where(is_first | is_last, 1.0, 2.0).astype(jnp.float32)
        ahead = jnp.where(stage == 2, STEP_SIZE, 0.5 * STEP_SIZE).astype(jnp.float32)

        def update(i):
            y = oprod[h, i] + gprod[h, numbers[gsum_at + i]]
            for k in range(members):
                y = y + zprod[h, numbers[zsum_at + i * members + k]]
            v = field[h, i]
            u = out[i, part, :]
            slope = rate[pl.ds(i, 1), :] * (v - v * v * v) - y
            before = jnp.where(is_first, 0.0, total[h, i])
            summed = before + weight * slope
            total[h, i] = summed
            value = u + jnp.where(is_last, (STEP_SIZE / 6.0) * summed, ahead * slope)
            out[i, part, :] = jnp.where(is_last, value, u)
            field[h, i] = value
            own[h, i] = value.astype(jnp.bfloat16)

        def four(n, _):
            for i in range(4):
                update(n * 4 + i)
            return 0

        lax.fori_loop(0, rows // 4, four, 0)
        pl.when(e + 1 < EVALS)(lambda: launch(e + 1, h))

    copies = [table_copy(side_, t) for t in range(1, DEPTH + 1) for side_ in (0, 1)]
    for copy in copies:
        copy.start()

    def open_part(h, _):
        first(h)
        launch(0, h)
        return 0

    lax.fori_loop(0, PARTS, open_part, 0)
    for copy in copies:
        copy.wait_recv()
    fetch = pltpu.make_async_copy(table_in, table, load_sem.at[1])
    fetch.start()
    fetch.wait()
    for copy in copies:
        copy.wait_send()
    load.wait()

    turns = PARTS * EVALS

    def turn(n, _):
        def at(lag, last, what):
            k = n - lag

            def run():
                what(lax.div(k, PARTS), lax.rem(k, PARTS))

            pl.when((k >= 0) & (k < last))(run)

        for name, lag in ORDER:
            if name == "turn":
                pl.when(n >= PARTS)(lambda: finish(lax.div(n, PARTS) - 1, lax.rem(n, PARTS)))
                at(0, turns, begin)
            elif name == "across":
                at(lag, turns, across)
            elif name == "group":
                at(lag, turns, group_products)
            else:
                at(lag, turns, lambda e, h, t=int(name): step(e, h, t))
        return 0

    lax.fori_loop(0, turns + PARTS, turn, 0)


def per_device(groups, state, blocks, rate, own_col, member_col, group_col, member_send, group_send):
    rows, traj, cells = state.shape
    members = member_col.shape[1]
    count = blocks.shape[1]
    per_group = group_send.shape[1] // groups
    part = traj // PARTS
    half, nears = Z // 2, 2 * DEPTH + 1
    g = lax.axis_index("group")
    m = lax.axis_index("member")
    x, z = m // Z, m % Z

    col = member_col.reshape(-1)
    zsum = ((x - col // Z + X) % X) * Z + slot_of((z - col % Z + Z) % Z)
    ids = jnp.arange(rows * members, dtype=jnp.int32)
    block_of = (ids // members) * count + 1 + ids % members
    zblk = jnp.sum(jnp.where(zsum[None, :] == ids[:, None], block_of[None, :], 0), axis=1)
    gcol = group_col.reshape(-1)
    gsum = ((g - gcol // per_group + groups) % groups) * per_group + gcol % per_group
    gids = jnp.arange(gcol.shape[0], dtype=jnp.int32)
    gblock = gids * count + count - 1
    gblk = jnp.sum(jnp.where(gsum[None, :] == gids[:, None], gblock[None, :], 0), axis=1)

    numbers = jnp.concatenate(
        [zblk, zsum, gblk, gsum, own_col, group_send[0], member_send[0]]
    ).astype(jnp.int32)
    own_table = jnp.pad(member_send, ((0, 0), (0, -member_send.shape[1] % cells)))

    smem = pl.BlockSpec(memory_space=pltpu.SMEM)
    vmem = pl.BlockSpec(memory_space=pltpu.VMEM)
    bf, f32 = jnp.bfloat16, jnp.float32
    tile = (part, cells)
    dma = pltpu.SemaphoreType.DMA
    return pl.pallas_call(
        functools.partial(kernel, groups, rows, per_group),
        out_shape=jax.ShapeDtypeStruct(state.shape, f32),
        in_specs=[smem, vmem, vmem, pl.BlockSpec(memory_space=pl.ANY), vmem],
        out_specs=vmem,
        scratch_shapes=[
            pltpu.VMEM((rows * count, cells, cells), bf),
            pltpu.VMEM((2 * DEPTH,) + own_table.shape, jnp.int32),
            pltpu.SMEM((2 * DEPTH,) + own_table.shape, jnp.int32),
            dma((2 * DEPTH,)),
            dma((2 * DEPTH,)),
            dma((2,)),
            pltpu.VMEM((PARTS, rows) + tile, bf),
            pltpu.VMEM((PARTS, rows) + tile, f32),
            pltpu.VMEM((PARTS, rows) + tile, f32),
            pltpu.VMEM((2, PARTS, 2, DEPTH, rows) + tile, bf),
            pltpu.VMEM((rows,) + tile, bf),
            pltpu.VMEM((rows,) + tile, bf),
            pltpu.VMEM((PARTS, X, nears) + tile, bf),
            pltpu.VMEM((2, PARTS, X, Z - nears) + tile, bf),
            pltpu.VMEM((2, PARTS, X - 1, Z) + tile, bf),
            pltpu.VMEM((PARTS, 2, half - DEPTH, X) + tile, bf),
            pltpu.VMEM((PARTS, groups * per_group) + tile, bf),
            pltpu.VMEM((2, PARTS, (groups - 1) * per_group) + tile, bf),
            pltpu.VMEM((PARTS, X * Z) + tile, f32),
            pltpu.VMEM((PARTS, groups * per_group) + tile, f32),
            pltpu.VMEM((PARTS, rows) + tile, f32),
            dma((PARTS, 2, DEPTH)),
            dma((2, PARTS, 2, DEPTH)),
            dma((PARTS, 2, half - DEPTH)),
            dma((2, PARTS, 2, half - DEPTH)),
            dma((PARTS, X - 1)),
            dma((2, PARTS, X - 1)),
            dma((PARTS, X - 1)),
            dma((2, PARTS, X - 1)),
            dma((PARTS, groups - 1)),
            dma((2, PARTS, groups - 1)),
        ],
        compiler_params=pltpu.CompilerParams(
            collective_id=0, has_side_effects=True, vmem_limit_bytes=60 * 2**20
        ),
        cost_estimate=pl.CostEstimate(
            flops=EVALS * 2 * rows * count * traj * cells * cells,
            bytes_accessed=4 * 2**20, transcendentals=0,
        ),
    )(
        numbers, own_table, state, blocks.reshape(rows * count, cells, cells), rate,
    )


def solution(mesh):
    return jax.shard_map(
        functools.partial(per_device, mesh.shape["group"]),
        mesh=mesh,
        in_specs=(
            P(("group", "member"), None, None),
            P(("group", "member"), None, None, None),
            P(("group", "member"), None),
            P(("group", "member")),
            P(("group", "member"), None),
            P(("group", "member"), None),
            P(("group", "member"), None),
            P(("group", "member"), None),
        ),
        out_specs=P(("group", "member"), None, None),
        check_vma=False,
    )
```

time: 463 us -> 317 us (0.68)
  blocking collectives: 78.7 us -> 0 us
  Pallas kernels: 376 us -> 310 us
    all_gather x1 -> x0, blocking collectives: 78.7 us -> none  [per_device(): table = lax.all_gather(member_send[0], 'member', axis=0)]
    pallas_call x1, Pallas kernels: 376 us -> 310 us  [per_device(): pl.pallas_call(functools.partial(kernel, groups, rows, per_group), out_sh...]
where the time goes in v2:
time: 317 us; the launch traced here: 316 us
  Pallas kernels  310 us (98%)
  local copies, waits for them, and re-layouts  5.32 us (2%)
    pallas_call x1, Pallas kernels, per_device(): pl.pallas_call(functools.partial(kernel, groups, rows, per_group), out_sh...  310 us

profile of v2, /device:TPU:6, one launch (start us, length us, event | category | flops | bytes accessed | tf_op | source)
XLA Modules:
  0.0 316.1 jit_solution(17440968781666234689)
XLA Ops:
  0.0 1.3 pad.4.own_table
  1.3 0.7 fusion.1
  1.9 0.1 select_reduce_fusion.1
  2.0 0.8 copy.11
  2.8 0.1 reshape.190
  2.9 0.1 select_reduce_fusion
  3.0 1.3 concatenate.3.numbers
  4.4 309.8 %shard_map.82 = f32[16,64,128]{2,1,0:T(8,128)} custom-call(s32[256]{0:T(256)} %concatenate.3.numbers, s32[1,128]{1,0:T(1,128)} %pad.4.own_table, f32[16,64,128]{2,1,0:T(8,128)} %state.1, bf16[96,128,128]{2,1,0:T(8,128)(2,1)} %bitcast.18, f32[16,128]{1,0:T(8,128)} %rate.1), custom_call_target="tpu_custom_call" | custom-call | flops 1610612736 | bytes 4194304 | tf_op jit(solution)/shard_map/pallas_call | solution.py:366
  314.2 1.9 copy.13
  (1 shorter events, 0.0 us)
